TPU v7x, 32 devices: a whole 2x2x4 slice. The times are simulated.
32 devices in a mesh: groups: 2 (over y), inp: 8 (over z, x), out: 2 (over core).
Axes of the slice: x: 2, y: 2, z: 4, core: 2. Of those that a mesh axis runs over, the one named last changes fastest.
Arguments:
- tokens: bfloat16 [16, 16384], P('groups', 'inp'), parts along dimension 0, may hold values from -6 to 6
- norm_gain: bfloat16 [16384], P('inp'), may hold values from 0.5 to 1.5
- positions: int32 [16], P('groups'), parts along dimension 0, may hold values from 0 to 7, as said below
- w_query: bfloat16 [16384, 8192], P('inp', 'out'), may hold values from -0.046875 to 0.046875
- key_weight: bfloat16 [16384, 512], P('inp', 'out'), may hold values from -0.046875 to 0.046875
- value_weight: bfloat16 [16384, 512], P('inp', 'out'), may hold values from -0.046875 to 0.046875
- w_output: bfloat16 [8192, 16384], P('out', 'inp'), may hold values from -0.25 to 0.25
Outputs:
- block_out: bfloat16 [16, 16384], P(('groups', 'out'), 'inp'), parts along dimension 0
There are 2 independent parts, one for each index of `groups`. A program takes and returns all parts, laid end to end along the dimension named above; an argument that names none is the same for every part. Nothing has to cross between parts.
Inputs may be any that keep to these rules, and one draw needn't show every extreme that they name: `positions`: each entry is either 0 (a new document) or one more than the entry before it; the stretch's first document covers more than 4 tokens and ends at position 7.
All inputs are finite; a program needn't handle non-finite values.
Results may differ from a plain program's by a relative error of at most 0.0071.
Values may be sent and summed in bfloat16 or wider, within the bound.
A program may use at most 128 MiB of HBM per device.

v0:
```python
import jax
import jax.numpy as jnp
from jax import lax
from jax.sharding import PartitionSpec as P

MODEL_WIDTH = 16384
HEAD_SIZE = 128


THETA = 500000.0


def apply_rotary(flat, pos):
    rows = flat.shape[0]
    heads = flat.shape[1] // HEAD_SIZE
    half = HEAD_SIZE // 2
    shaped = flat.astype(jnp.float32).reshape(rows, heads, HEAD_SIZE)
    index_f = jnp.arange(half, dtype=jnp.float32)
    freq = jnp.exp(-jnp.log(jnp.float32(THETA)) * 2.0 * index_f / (2.0 * half))
    angle = pos.astype(jnp.float32)[:, None] * freq[None, :]
    cosine = jnp.cos(angle)[:, None, :]
    sine = jnp.sin(angle)[:, None, :]
    first = shaped[..., :half]
    second = shaped[..., half:]
    turned = jnp.concatenate(
        [first * cosine - second * sine, second * cosine + first * sine], axis=-1
    )
    return turned.reshape(rows, heads * HEAD_SIZE).astype(jnp.bfloat16)


def attend(rotated_query, row_pos, row_index, rotated_keys, value_matrix):
    rows = rotated_query.shape[0]
    partial_total = rotated_keys.shape[0]
    kv_heads = rotated_keys.shape[1] // HEAD_SIZE
    query_group = rotated_query.shape[1] // HEAD_SIZE // kv_heads
    q_shaped = rotated_query.reshape(rows, kv_heads, query_group, HEAD_SIZE)
    k_shaped = rotated_keys.reshape(partial_total, kv_heads, HEAD_SIZE)
    v_shaped = value_matrix.reshape(partial_total, kv_heads, HEAD_SIZE)
    scores = jnp.einsum("rkgd,skd->rkgs", q_shaped, k_shaped, preferred_element_type=jnp.float32)
    scores = scores / jnp.sqrt(jnp.float32(HEAD_SIZE))
    cols = jnp.arange(partial_total, dtype=jnp.int32)[None, :]
    allowed = (cols <= row_index[:, None]) & (row_index[:, None] - cols <= row_pos[:, None])
    scores = jnp.where(allowed[:, None, None, :], scores, jnp.float32(-1e30))
    expo = jnp.exp(scores)
    probs = (expo / jnp.sum(expo, axis=-1, keepdims=True)).astype(jnp.bfloat16)
    context = jnp.einsum("rkgs,skd->rkgd", probs, v_shaped, preferred_element_type=jnp.float32)
    return context.astype(jnp.bfloat16).reshape(rows, kv_heads * query_group * HEAD_SIZE)


def shards(tokens, norm_gain, positions, w_query, key_weight, value_weight, w_output):
    partial_total = tokens.shape[0]
    token_f = tokens.astype(jnp.float32)
    squares = lax.psum(jnp.sum(token_f * token_f, axis=1), "inp")
    scale = lax.rsqrt(squares / MODEL_WIDTH + 1e-05)
    normed = (token_f * scale[:, None] * norm_gain.astype(jnp.float32)[None, :]).astype(
        jnp.bfloat16
    )
    query_width = w_query.shape[1]
    q_part = jnp.dot(normed, w_query, preferred_element_type=jnp.float32)
    k_part = jnp.dot(normed, key_weight, preferred_element_type=jnp.float32)
    v_part = jnp.dot(normed, value_weight, preferred_element_type=jnp.float32)
    q_sum, k_sum, v_sum = lax.psum((q_part, k_part, v_part), "inp")
    rotated_query = apply_rotary(q_sum.astype(jnp.bfloat16), positions)
    rotated_keys = apply_rotary(k_sum.astype(jnp.bfloat16), positions)
    value_matrix = v_sum.astype(jnp.bfloat16)
    block_rows = min(partial_total, 128)
    blocks = partial_total // block_rows
    index_all = jnp.arange(partial_total, dtype=jnp.int32)

    def one_block(packed):
        q_block, pos_block, index_block = packed
        return attend(q_block, pos_block, index_block, rotated_keys, value_matrix)

    context = lax.map(
        one_block,
        (
            rotated_query.reshape(blocks, block_rows, query_width),
            positions.reshape(blocks, block_rows),
            index_all.reshape(blocks, block_rows),
        ),
    )
    context = context.reshape(partial_total, query_width)
    partial_out = jnp.dot(context, w_output, preferred_element_type=jnp.float32)
    reduced = lax.psum_scatter(partial_out, "out", scatter_dimension=0, tiled=True)
    half_rows = reduced.shape[0]
    residual = lax.dynamic_slice_in_dim(token_f, lax.axis_index("out") * half_rows, half_rows, 0)
    return (reduced + residual).astype(jnp.bfloat16)


def solution(mesh):
    return jax.shard_map(
        shards,
        mesh=mesh,
        in_specs=(
            P("groups", "inp"),
            P("inp"),
            P("groups"),
            P("inp", "out"),
            P("inp", "out"),
            P("inp", "out"),
            P("out", "inp"),
        ),
        out_specs=P(("groups", "out"), "inp"),
        check_vma=False,
    )
```

profile of v0, /device:TPU:0, one launch (start us, length us, event | category | flops | bytes accessed | tf_op | source)
XLA Modules:
  0.0 111.0 jit_solution(11003973649414624287)
XLA Ops:
  6.5 0.0 copy-start
  6.5 0.0 copy-start.2
  6.5 0.0 copy-start.1
  6.5 0.0 all-reduce.5.cloned.1.call-start
  6.6 0.8 convert_element_type.50
  7.4 0.7 fusion.15
  8.1 0.9 multiply_reduce_fusion
  9.0 0.7 convert_element_type.46
  9.7 23.1 %psum.28 = f32[8]{0:T(128)S(1)} all-reduce(f32[8]{0:T(128)S(1)} %multiply_reduce_fusion), channel_id=1, replica_groups=mesh['groups'=2,'inp'=8,'out'=2] {'inp'}, use_global_device_ids=true, to_apply=%region_1.0 | all-reduce | flops 8 | bytes 64 | tf_op jit(solution)/shard_map/psum | solution.py:53
  32.8 8.1 %fusion.21 = f32[8,4096]{1,0:T(8,128)S(1)} fusion(bf16[2048,4096]{1,0:T(8,128)(2,1)} %param.10, f32[2048]{0:T(1024)S(1)} %convert_element_type.46, f32[8]{0:T(128)S(1)} %add_rsqrt_fusion, bf16[8,2048]{1,0:T(8,128)(2,1)} %param.7), kind=kOutput, calls=%fused_computation.38 | convolution fusion | flops 134283264 | bytes 16949280 | tf_op jit(solution)/shard_map/dot_general | solution.py:59
  40.9 0.0 copy-done
  40.9 0.0 copy-done.2
  40.9 0.0 copy-start.3
  40.9 0.3 fusion.22
  41.2 0.0 copy-done.1
  41.2 0.3 fusion.23
  41.4 34.7 %all-reduce.6 = (bf16[8,4096]{1,0:T(8,128)(2,1)S(1)}, bf16[8,256]{1,0:T(8,128)(2,1)S(1)}, bf16[8,256]{1,0:T(8,128)(2,1)S(1)}) all-reduce(f32[8,4096]{1,0:T(8,128)S(1)} %fusion.21, f32[8,256]{1,0:T(8,128)S(1)} %fusion.22, f32[8,256]{1,0:T(8,128)S(1)} %fusion.23), channel_id=1, replica_groups=mesh['groups'=2,'inp'=8,'out'=2] {'inp'}, use_global_device_ids=true, to_apply=%region_4.0 | all-reduce | flops 36864 | bytes 221184 | tf_op jit(solution)/shard_map/psum | solution.py:62
  76.2 0.1 fusion.24
  76.3 0.1 multiply_cosine_fusion
  76.4 0.1 subtract_convert_fusion.1
  76.5 0.1 subtract_convert_fusion
  76.5 0.1 pad_maximum_fusion
  76.6 0.3 fusion.3
  76.9 0.2 fusion
  77.2 8.7 %fusion.4 = f32[8,2048]{1,0:T(8,128)} fusion(bf16[4096,2048]{1,0:T(8,128)(2,1)} %param.13, bf16[1,8,32,128]{3,2,1,0:T(8,128)(2,1)S(1)} %bitcast.42), kind=kOutput, calls=%fused_computation.8 | convolution fusion | flops 134217728 | bytes 16908288 | tf_op jit(solution)/shard_map/dot_general | solution.py:83
  85.8 0.0 all-reduce.5.cloned.1.call-update
  85.9 0.0 copy-done.3
  85.9 0.6 dynamic-slice.2
  87.1 15.6 %all-reduce.5.cloned.1.call-done = f32[8,2048]{1,0:T(8,128)} async-done(((f32[8,2048]{1,0:T(8,128)}), f32[8,2048]{1,0:T(8,128)}) %all-reduce.5.cloned.1.call-update) | async-done | bytes 65552
  102.7 1.5 %fusion.8 = bf16[4,2048]{1,0:T(4,128)(2,1)} fusion(f32[8,2048]{1,0:T(8,128)} %all-reduce.5.cloned.1.call-done, u32[]{:T(128)S(6)} %multiply.11, f32[8,2048]{1,0:T(8,128)S(1)} %convert_element_type.45, s32[]{:T(128)S(6)} %select_n.9), kind=kLoop, calls=%fused_computation.18 | loop fusion | flops 16384 | bytes 81928 | tf_op jit(solution)/shard_map/convert_element_type | solution.py:87
  (6 shorter events, 0.0 us)
Async XLA Ops:
  6.5 34.3 %copy-start = (bf16[2048,256]{1,0:T(8,128)(2,1)S(1)}, bf16[2048,256]{1,0:T(8,128)(2,1)}, u32[]{:S(2)}) copy-start(bf16[2048,256]{1,0:T(8,128)(2,1)} %param.11) | copy-start | bytes 3145732
  6.5 34.3 %copy-start.2 = (bf16[8,2048]{1,0:T(8,128)(2,1)S(1)}, bf16[8,2048]{1,0:T(8,128)(2,1)}, u32[]{:S(2)}) copy-start(bf16[8,2048]{1,0:T(8,128)(2,1)} %param.7) | copy-start | bytes 98308
  6.5 34.6 %copy-start.1 = (bf16[2048,256]{1,0:T(8,128)(2,1)S(1)}, bf16[2048,256]{1,0:T(8,128)(2,1)}, u32[]{:S(2)}) copy-start(bf16[2048,256]{1,0:T(8,128)(2,1)} %param.12) | copy-start | bytes 3145732
  6.5 96.2 %all-reduce.5.cloned.1.call-start = ((), (), s32[]{:S(2)}) async-start(), calls=%async_computation | async-start | bytes 131072
  40.9 45.0 %copy-start.3 = (u32[32]{0:T(128)S(1)}, u32[32]{0:T(128)}, u32[]{:S(2)}) copy-start(u32[32]{0:T(128)} %constant.45) | copy-start | bytes 388
Sparse Core Ops, SparseCore 0:
  86.0 16.6 all-reduce.4
where the time goes:
time: 111 us
  blocking collectives  57.8 us (52%)
  matrix products  17.9 us (16%)
  waiting for transfers between devices  15.6 us (14%)
  between operations  14.1 us (13%)
  other arithmetic  4.95 us (4%)
    psum x1, blocking collectives, shards(): q_sum, k_sum, v_sum = lax.psum((q_part, k_part, v_part), 'inp')  34.7 us
    psum x1, blocking collectives, shards(): squares = lax.psum(jnp.sum(token_f * token_f, axis=1), 'inp')  23.1 us
    unnamed x2, waiting for transfers between devices  15.6 us
    dot_general x1, matrix products, shards(): partial_out = jnp.dot(context, w_output, preferred_element_type=jnp.float32)  8.67 us
    dot_general x1, matrix products, shards(): q_part = jnp.dot(normed, w_query, preferred_element_type=jnp.float32)  8.1 us
  transfers between devices with their start and end apart: 1, of which 1 were waited for; matrix products, arithmetic and copies ran while one was open for 1% of the time, Pallas kernels for 0%

commit v1 on v0

--- a/solution.py
+++ b/solution.py
@@ -1,6 +1,11 @@
+import functools
+import math
+
 import jax
 import jax.numpy as jnp
 from jax import lax
+from jax.experimental import pallas as pl
+from jax.experimental.pallas import tpu as pltpu
 from jax.sharding import PartitionSpec as P
 
 MODEL_WIDTH = 16384
@@ -87,9 +92,330 @@
     return (reduced + residual).astype(jnp.bfloat16)
 
 
+MESH = pl.DeviceIdType.MESH
+
+
+def neighbour_at(me, step, count):
+    offset = ((step + 1) // 2) * (2 * (step % 2) - 1)
+    return (me + offset + count) % count
+
+
+def fused_kernel(
+    count,
+    pos_ref,
+    tok_ref,
+    gain_ref,
+    wq_hbm,
+    wk_hbm,
+    wv_hbm,
+    wo_hbm,
+    out_ref,
+    wq,
+    wkv,
+    wo,
+    x_buf,
+    kv_buf,
+    squares,
+    part_out,
+    part_in,
+    own_part,
+    ctx_all,
+    swap_out,
+    swap_in,
+    wq_sem,
+    wkv_sem,
+    wo_sem,
+    sq_send,
+    sq_recv,
+    part_send,
+    part_recv,
+    ctx_send,
+    ctx_recv,
+    swap_sem,
+):
+    me = lax.axis_index("inp")
+    core = lax.axis_index("out")
+    rows = tok_ref.shape[0]
+    width = wq.shape[2]
+    heads = width // HEAD_SIZE
+    kv_width = wk_hbm.shape[1]
+    kv_heads = kv_width // HEAD_SIZE
+    per_kv = count // kv_heads
+
+    def wq_copy(chunk):
+        cols = pl.ds(pl.multiple_of(chunk * width, width), width)
+        return pltpu.make_async_copy(wq_hbm.at[:, cols], wq.at[chunk], wq_sem.at[chunk])
+
+    def wo_copy(chunk):
+        at = pl.ds(pl.multiple_of(chunk * width, width), width)
+        return pltpu.make_async_copy(wo_hbm.at[at, :], wo.at[chunk], wo_sem.at[chunk])
+
+    def wk_copy():
+        return pltpu.make_async_copy(wk_hbm, wkv.at[:, 0:kv_width], wkv_sem.at[0])
+
+    def wv_copy():
+        return pltpu.make_async_copy(wv_hbm, wkv.at[:, kv_width : 2 * kv_width], wkv_sem.at[1])
+
+    def sq_copy(other):
+        return pltpu.make_async_remote_copy(
+            src_ref=squares.at[me],
+            dst_ref=squares.at[me],
+            send_sem=sq_send.at[other],
+            recv_sem=sq_recv.at[me],
+            device_id={"inp": other},
+            device_id_type=MESH,
+        )
+
+    def part_copy(other):
+        return pltpu.make_async_remote_copy(
+            src_ref=part_out.at[other],
+            dst_ref=part_in.at[me],
+            send_sem=part_send.at[other],
+            recv_sem=part_recv.at[me],
+            device_id={"inp": other},
+            device_id_type=MESH,
+        )
+
+    def ctx_copy(other):
+        return pltpu.make_async_remote_copy(
+            src_ref=ctx_all.at[me],
+            dst_ref=ctx_all.at[me],
+            send_sem=ctx_send.at[other],
+            recv_sem=ctx_recv.at[me],
+            device_id={"inp": other},
+            device_id_type=MESH,
+        )
+
+    def arrival(buffer, send, recv, other):
+        return pltpu.make_async_remote_copy(
+            src_ref=buffer.at[other],
+            dst_ref=buffer.at[other],
+            send_sem=send.at[other],
+            recv_sem=recv.at[other],
+            device_id={"inp": other},
+            device_id_type=MESH,
+        )
+
+    wk_copy().start()
+    wv_copy().start()
+    for step in range(count - 1, -1, -1):
+        wq_copy(neighbour_at(me, step, count)).start()
+
+    barrier = pltpu.get_barrier_semaphore()
+    for step in range(1, count):
+        other = neighbour_at(me, step, count)
+        pl.semaphore_signal(barrier, inc=1, device_id={"inp": other}, device_id_type=MESH)
+    pl.semaphore_signal(barrier, inc=1, device_id={"out": 1 - core}, device_id_type=MESH)
+
+    token_f = tok_ref[...].astype(jnp.float32)
+    gain = gain_ref[...].astype(jnp.float32)
+    x_buf[...] = (token_f * gain).astype(jnp.bfloat16)
+    squares[me] = jnp.broadcast_to(
+        jnp.sum(token_f * token_f, axis=1, keepdims=True), (rows, HEAD_SIZE)
+    )
+
+    pl.semaphore_wait(barrier, count)
+    for step in range(count - 1, 0, -1):
+        sq_copy(neighbour_at(me, step, count)).start()
+
+    half = HEAD_SIZE // 2
+    row_at = lax.broadcasted_iota(jnp.int32, (rows, HEAD_SIZE), 0)
+    lane_at = lax.broadcasted_iota(jnp.int32, (rows, HEAD_SIZE), 1)
+    position = jnp.zeros((rows, HEAD_SIZE), jnp.int32)
+    for row in range(rows):
+        position = jnp.where(row_at == row, pos_ref[row], position)
+    index_f = jnp.where(lane_at < half, lane_at, lane_at - half).astype(jnp.float32)
+    freq = jnp.exp(index_f * jnp.float32(-2.0 * math.log(THETA) / HEAD_SIZE))
+    angle = position.astype(jnp.float32) * freq
+    cosine = jnp.cos(angle)
+    sine = jnp.sin(angle)
+    sine = jnp.where(lane_at < half, -sine, sine)
+
+    def rotate(block):
+        return (block * cosine + pltpu.roll(block, half, 1) * sine).astype(jnp.bfloat16)
+
+    wk_copy().wait()
+    wv_copy().wait()
+    kv_part = jnp.dot(x_buf[...], wkv[...], preferred_element_type=jnp.float32)
+    for head in range(kv_heads):
+        kv_buf[head, :, 0:HEAD_SIZE] = kv_part[:, head * HEAD_SIZE : (head + 1) * HEAD_SIZE]
+        kv_buf[head, :, HEAD_SIZE : 2 * HEAD_SIZE] = kv_part[
+            :, kv_width + head * HEAD_SIZE : kv_width + (head + 1) * HEAD_SIZE
+        ]
+
+    def project(chunk):
+        wq_copy(chunk).wait()
+        wo_copy(chunk).start()
+        q_part = jnp.dot(x_buf[...], wq[chunk], preferred_element_type=jnp.float32)
+        whole = jnp.concatenate([q_part, kv_buf[chunk // per_kv]], axis=1)
+        cut = whole.shape[1] // 2
+        return jnp.concatenate([whole[:, :cut], whole[:, cut:]], axis=0)
+
+    def project_step(at, carry):
+        other = neighbour_at(me, count - 1 - at, count)
+        part_out[other] = project(other).astype(jnp.bfloat16)
+        part_copy(other).start()
+        return carry
+
+    lax.fori_loop(0, count - 1, project_step, 0)
+    own_part[...] = project(me)
+
+    for step in range(1, count):
+        arrival(squares, sq_send, sq_recv, neighbour_at(me, step, count)).wait_recv()
+    total_sq = squares[0]
+    for at in range(1, count):
+        total_sq = total_sq + squares[at]
+    scale = lax.rsqrt(total_sq / MODEL_WIDTH + 1e-05)
+
+    total = own_part[...]
+    for step in range(1, count):
+        other = neighbour_at(me, step, count)
+        arrival(part_in, part_send, part_recv, other).wait_recv()
+        total = total + part_in[other].astype(jnp.float32)
+    blocks = []
+    for side in range(2):
+        for at in range(total.shape[1] // HEAD_SIZE):
+            piece = total[side * rows : (side + 1) * rows, at * HEAD_SIZE : (at + 1) * HEAD_SIZE]
+            blocks.append((piece * scale).astype(jnp.bfloat16).astype(jnp.float32))
+    query = jnp.concatenate([rotate(blocks[head]) for head in range(heads)], axis=0)
+    keys = rotate(blocks[heads])
+    values = blocks[heads + 1].astype(jnp.bfloat16)
+    scores = lax.dot_general(
+        query, keys, (((1,), (1,)), ((), ())), preferred_element_type=jnp.float32
+    ) / math.sqrt(HEAD_SIZE)
+    cols = lane_at[:, :rows]
+    distance = row_at[:, :rows] - cols
+    allowed = jnp.where((distance >= 0) & (distance <= position[:, :rows]), 1.0, 0.0)
+    allowed = jnp.concatenate([allowed] * heads, axis=0)
+    expo = jnp.exp(jnp.where(allowed > 0.5, scores, -1e30))
+    probs = (expo / jnp.sum(expo, axis=1, keepdims=True)).astype(jnp.bfloat16)
+    context = jnp.dot(probs, values, preferred_element_type=jnp.float32)
+    half_heads = heads // 2
+    sides = [
+        jnp.concatenate(
+            [
+                context[(side * half_heads + at) * rows : (side * half_heads + at + 1) * rows]
+                for at in range(half_heads)
+            ],
+            axis=1,
+        )
+        for side in range(2)
+    ]
+    ctx_all[me] = jnp.concatenate(sides, axis=0).astype(jnp.bfloat16)
+    for step in range(count - 1, 0, -1):
+        ctx_copy(neighbour_at(me, step, count)).start()
+
+    def contribution(chunk):
+        wo_copy(chunk).wait()
+        packed = ctx_all[chunk].astype(jnp.float32)
+        left = jnp.concatenate([packed[:rows], packed[rows:]], axis=1).astype(jnp.bfloat16)
+        return jnp.dot(left, wo[chunk], preferred_element_type=jnp.float32)
+
+    def output_step(step, acc):
+        other = neighbour_at(me, step, count)
+        arrival(ctx_all, ctx_send, ctx_recv, other).wait_recv()
+        return acc + contribution(other)
+
+    acc = lax.fori_loop(1, count, output_step, contribution(me))
+
+    def pack(array, keep):
+        cut = array.shape[1] // 2
+        low, high = array[:, :cut], array[:, cut:]
+        upper = lax.broadcasted_iota(jnp.int32, low.shape, 0) < rows // 2
+        first = jnp.where(upper, low, pltpu.roll(high, rows // 2, 0))
+        second = jnp.where(upper, pltpu.roll(low, rows // 2, 0), high)
+        return jnp.where(keep == 0, first, second)
+
+    swap_out[...] = pack(acc, 1 - core)
+    swap = pltpu.make_async_remote_copy(
+        src_ref=swap_out,
+        dst_ref=swap_in,
+        send_sem=swap_sem.at[0],
+        recv_sem=swap_sem.at[1],
+        device_id={"out": 1 - core},
+        device_id_type=MESH,
+    )
+    swap.start()
+    mine = pack(acc, core)
+    residual = pack(tok_ref[...].astype(jnp.float32), core)
+    swap.wait_recv()
+    result = (mine + swap_in[...] + residual).astype(jnp.bfloat16)
+    cut = result.shape[1]
+    out_ref[:, :cut] = result[: rows // 2]
+    out_ref[:, cut:] = result[rows // 2 :]
+
+    swap.wait_send()
+    for step in range(1, count):
+        other = neighbour_at(me, step, count)
+        sq_copy(other).wait_send()
+        part_copy(other).wait_send()
+        ctx_copy(other).wait_send()
+
+
+def fused(count, tokens, norm_gain, positions, w_query, key_weight, value_weight, w_output):
+    rows, depth = tokens.shape
+    query_width = w_query.shape[1]
+    width = query_width // count
+    kv_width = key_weight.shape[1]
+    out_width = w_output.shape[1]
+    packed = (width + 2 * HEAD_SIZE) // 2
+    hbm = pl.BlockSpec(memory_space=pl.ANY)
+    vmem = pl.BlockSpec(memory_space=pltpu.VMEM)
+    dma = pltpu.SemaphoreType.DMA
+    return pl.pallas_call(
+        functools.partial(fused_kernel, count),
+        out_shape=jax.ShapeDtypeStruct((rows // 2, out_width), jnp.bfloat16),
+        in_specs=[pl.BlockSpec(memory_space=pltpu.SMEM), vmem, vmem, hbm, hbm, hbm, hbm],
+        out_specs=vmem,
+        scratch_shapes=[
+            pltpu.VMEM((count, depth, width), jnp.bfloat16),
+            pltpu.VMEM((depth, 2 * kv_width), jnp.bfloat16),
+            pltpu.VMEM((count, width, out_width), jnp.bfloat16),
+            pltpu.VMEM((rows, depth), jnp.bfloat16),
+            pltpu.VMEM((kv_width // HEAD_SIZE, rows, 2 * HEAD_SIZE), jnp.float32),
+            pltpu.VMEM((count, rows, HEAD_SIZE), jnp.float32),
+            pltpu.VMEM((count, 2 * rows, packed), jnp.bfloat16),
+            pltpu.VMEM((count, 2 * rows, packed), jnp.bfloat16),
+            pltpu.VMEM((2 * rows, packed), jnp.float32),
+            pltpu.VMEM((count, 2 * rows, width // 2), jnp.bfloat16),
+            pltpu.VMEM((rows, out_width // 2), jnp.float32),
+            pltpu.VMEM((rows, out_width // 2), jnp.float32),
+            dma((count,)),
+            dma((2,)),
+            dma((count,)),
+            dma((count,)),
+            dma((count,)),
+            dma((count,)),
+            dma((count,)),
+            dma((count,)),
+            dma((count,)),
+            dma((2,)),
+        ],
+        compiler_params=pltpu.CompilerParams(
+            collective_id=0, has_side_effects=True, vmem_limit_bytes=56 * 1024 * 1024
+        ),
+    )(positions, tokens, norm_gain.reshape(1, depth), w_query, key_weight, value_weight, w_output)
+
+
+def block(count, cores, tokens, norm_gain, positions, w_query, key_weight, value_weight, w_output):
+    rows, depth = tokens.shape
+    query_width = w_query.shape[1]
+    kv_heads = key_weight.shape[1] // HEAD_SIZE
+    held = 2 * (w_query.size + w_output.size + 2 * key_weight.size)
+    fits = (
+        rows == 8
+        and cores == 2
+        and query_width % (2 * HEAD_SIZE * count) == 0
+        and count % kv_heads == 0
+        and held <= 40 * 1024 * 1024
+    )
+    form = functools.partial(fused, count) if fits else shards
+    return form(tokens, norm_gain, positions, w_query, key_weight, value_weight, w_output)
+
+
 def solution(mesh):
     return jax.shard_map(
-        shards,
+        functools.partial(block, mesh.shape["inp"], mesh.shape["out"]),
         mesh=mesh,
         in_specs=(
             P("groups", "inp"),

time: 111 us -> 27.8 us (0.25)
  blocking collectives: 57.8 us -> 0 us
  Pallas kernels: 0 us -> 24.9 us
  matrix products: 17.9 us -> 0 us
  waiting for transfers between devices: 15.6 us -> 0 us
  between operations: 14.1 us -> 0.01 us
  other arithmetic: 4.95 us -> 0 us
  local copies, waits for them, and re-layouts: 0.7 us -> 2.62 us
    psum x2 -> x0, blocking collectives: 57.8 us -> none  [the longest x1 34.7 us: shards(): q_sum, k_sum, v_sum = lax.psum((q_part, k_part, v_part), 'inp')]
    pallas_call x0 -> x1, Pallas kernels: none -> 24.9 us  [fused(): pl.pallas_call(functools.partial(fused_kernel, count), out_shape=jax.Shap...]
    dot_general x6 -> x0, matrix products: 17.9 us -> none  [the longest x1 8.67 us: shards(): partial_out = jnp.dot(context, w_output, preferred_element_type=jnp.float32)]
    unnamed x2 -> x0, waiting for transfers between devices: 15.6 us -> none
    convert_element_type x4 -> x0, other arithmetic: 2.96 us -> none  [the longest x1 1.46 us: shards(): return (reduced + residual).astype(jnp.bfloat16)]
    reshape x0 -> x1, local copies, waits for them, and re-layouts: none -> 1.29 us  [fused(): norm_gain.reshape(1, depth)]
  transfers between devices with their start and end apart: 1 -> 0, of which waited for: 1 -> 0; matrix products, arithmetic and copies ran while one was open for 1% -> 0% of each run, Pallas kernels for 0% -> 0%
where the time goes in v1:
time: 27.8 us; the launch traced here: 27.5 us
  Pallas kernels  24.9 us (90%)
  local copies, waits for them, and re-layouts  2.62 us (9%)
    pallas_call x1, Pallas kernels, fused(): pl.pallas_call(functools.partial(fused_kernel, count), out_shape=jax.Shap...  24.9 us
    unnamed x1, local copies, waits for them, and re-layouts  1.33 us
    reshape x1, local copies, waits for them, and re-layouts, fused(): norm_gain.reshape(1, depth)  1.29 us

profile of v1, /device:TPU:0, one launch (start us, length us, event | category | flops | bytes accessed | tf_op | source)
XLA Modules:
  0.0 27.5 jit_solution(915815777604487529)
XLA Ops:
  0.0 1.3 %reshape.3.gain_ref = bf16[1,2048]{1,0:T(2,128)(2,1)} reshape(bf16[2048]{0:T(1024)(128)(2,1)} %param.8) | data formatting | bytes 8192 | tf_op jit(solution)/shard_map/reshape | solution.py:397
  1.3 24.9 %shard_map.73 = bf16[4,2048]{1,0:T(4,128)(2,1)} custom-call(s32[8]{0:T(128)} %pos_ref.1, bf16[8,2048]{1,0:T(8,128)(2,1)} %tok_ref.1, bf16[1,2048]{1,0:T(2,128)(2,1)} %reshape.3.gain_ref, bf16[2048,4096]{1,0:T(8,128)(2,1)} %wq_hbm.1, bf16[2048,256]{1,0:T(8,128)(2,1)} %wk_hbm.1, bf16[2048,256]{1,0:T(8,128)(2,1)} %wv_hbm.1, bf16[4096,2048]{1,0:T(8,128)(2,1)} %wo_hbm.1), custom_call_target="tpu_custom_call" | custom-call | tf_op jit(solution)/shard_map/pallas_call | solution.py:365
  26.2 1.3 %copy.9 = bf16[4,2048]{1,0:T(4,128)(2,1)} copy(bf16[4,2048]{1,0:T(4,128)(2,1)} %shard_map.73) | data formatting | bytes 32768

commit v2 on v1

--- a/solution.py
+++ b/solution.py
@@ -102,20 +102,22 @@
 
 def fused_kernel(
     count,
-    pos_ref,
-    tok_ref,
-    gain_ref,
+    pos_hbm,
+    tok_hbm,
+    gain_hbm,
     wq_hbm,
     wk_hbm,
     wv_hbm,
     wo_hbm,
     out_ref,
+    pos_ref,
+    tok_ref,
+    gain_ref,
     wq,
     wkv,
     wo,
     x_buf,
     kv_buf,
-    squares,
     part_out,
     part_in,
     own_part,
@@ -125,8 +127,7 @@
     wq_sem,
     wkv_sem,
     wo_sem,
-    sq_send,
-    sq_recv,
+    small_sem,
     part_send,
     part_recv,
     ctx_send,
@@ -135,6 +136,7 @@
 ):
     me = lax.axis_index("inp")
     core = lax.axis_index("out")
+    partners = [neighbour_at(me, step, count) for step in range(count)]
     rows = tok_ref.shape[0]
     width = wq.shape[2]
     heads = width // HEAD_SIZE
@@ -155,16 +157,6 @@
 
     def wv_copy():
         return pltpu.make_async_copy(wv_hbm, wkv.at[:, kv_width : 2 * kv_width], wkv_sem.at[1])
-
-    def sq_copy(other):
-        return pltpu.make_async_remote_copy(
-            src_ref=squares.at[me],
-            dst_ref=squares.at[me],
-            send_sem=sq_send.at[other],
-            recv_sem=sq_recv.at[me],
-            device_id={"inp": other},
-            device_id_type=MESH,
-        )
 
     def part_copy(other):
         return pltpu.make_async_remote_copy(
@@ -196,27 +188,34 @@
             device_id_type=MESH,
         )
 
+    barrier = pltpu.get_barrier_semaphore()
+    for step in range(1, count):
+        other = partners[step]
+        pl.semaphore_signal(barrier, inc=1, device_id={"inp": other}, device_id_type=MESH)
+    pl.semaphore_signal(barrier, inc=1, device_id={"out": 1 - core}, device_id_type=MESH)
+
+    small = [
+        pltpu.make_async_copy(tok_hbm, tok_ref, small_sem.at[0]),
+        pltpu.make_async_copy(gain_hbm, gain_ref, small_sem.at[1]),
+        pltpu.make_async_copy(pos_hbm, pos_ref, small_sem.at[2]),
+    ]
+    for copy in small:
+        copy.start()
     wk_copy().start()
     wv_copy().start()
     for step in range(count - 1, -1, -1):
-        wq_copy(neighbour_at(me, step, count)).start()
-
-    barrier = pltpu.get_barrier_semaphore()
-    for step in range(1, count):
-        other = neighbour_at(me, step, count)
-        pl.semaphore_signal(barrier, inc=1, device_id={"inp": other}, device_id_type=MESH)
-    pl.semaphore_signal(barrier, inc=1, device_id={"out": 1 - core}, device_id_type=MESH)
-
+        wq_copy(partners[step]).start()
+
+    for copy in small:
+        copy.wait()
     token_f = tok_ref[...].astype(jnp.float32)
-    gain = gain_ref[...].astype(jnp.float32)
+    gain = gain_ref[...].astype(jnp.float32).reshape(1, -1)
     x_buf[...] = (token_f * gain).astype(jnp.bfloat16)
-    squares[me] = jnp.broadcast_to(
+    squares = jnp.broadcast_to(
         jnp.sum(token_f * token_f, axis=1, keepdims=True), (rows, HEAD_SIZE)
     )
-
-    pl.semaphore_wait(barrier, count)
-    for step in range(count - 1, 0, -1):
-        sq_copy(neighbour_at(me, step, count)).start()
+    high = squares.astype(jnp.bfloat16).astype(jnp.float32)
+    squares = jnp.concatenate([high, squares - high], axis=0)
 
     half = HEAD_SIZE // 2
     row_at = lax.broadcasted_iota(jnp.int32, (rows, HEAD_SIZE), 0)
@@ -249,32 +248,33 @@
         q_part = jnp.dot(x_buf[...], wq[chunk], preferred_element_type=jnp.float32)
         whole = jnp.concatenate([q_part, kv_buf[chunk // per_kv]], axis=1)
         cut = whole.shape[1] // 2
-        return jnp.concatenate([whole[:, :cut], whole[:, cut:]], axis=0)
-
-    def project_step(at, carry):
-        other = neighbour_at(me, count - 1 - at, count)
+        folded = jnp.concatenate([whole[:, :cut], whole[:, cut:]], axis=0)
+        return jnp.concatenate([folded, squares], axis=1)
+
+    early = min(2, count - 2)
+    for at in range(count - 1):
+        other = partners[count - 1 - at]
         part_out[other] = project(other).astype(jnp.bfloat16)
-        part_copy(other).start()
-        return carry
-
-    lax.fori_loop(0, count - 1, project_step, 0)
+        if at == early:
+            pl.semaphore_wait(barrier, count)
+            for before in range(early):
+                part_copy(partners[count - 1 - before]).start()
+        if at >= early:
+            part_copy(other).start()
     own_part[...] = project(me)
-
-    for step in range(1, count):
-        arrival(squares, sq_send, sq_recv, neighbour_at(me, step, count)).wait_recv()
-    total_sq = squares[0]
-    for at in range(1, count):
-        total_sq = total_sq + squares[at]
-    scale = lax.rsqrt(total_sq / MODEL_WIDTH + 1e-05)
 
     total = own_part[...]
     for step in range(1, count):
-        other = neighbour_at(me, step, count)
+        other = partners[step]
         arrival(part_in, part_send, part_recv, other).wait_recv()
         total = total + part_in[other].astype(jnp.float32)
+    columns = total.shape[1] // HEAD_SIZE - 1
+    total_sq = total[:, columns * HEAD_SIZE :]
+    total_sq = total_sq[:rows] + total_sq[rows:]
+    scale = lax.rsqrt(total_sq / MODEL_WIDTH + 1e-05)
     blocks = []
     for side in range(2):
-        for at in range(total.shape[1] // HEAD_SIZE):
+        for at in range(columns):
             piece = total[side * rows : (side + 1) * rows, at * HEAD_SIZE : (at + 1) * HEAD_SIZE]
             blocks.append((piece * scale).astype(jnp.bfloat16).astype(jnp.float32))
     query = jnp.concatenate([rotate(blocks[head]) for head in range(heads)], axis=0)
@@ -303,7 +303,7 @@
     ]
     ctx_all[me] = jnp.concatenate(sides, axis=0).astype(jnp.bfloat16)
     for step in range(count - 1, 0, -1):
-        ctx_copy(neighbour_at(me, step, count)).start()
+        ctx_copy(partners[step]).start()
 
     def contribution(chunk):
         wo_copy(chunk).wait()
@@ -311,12 +311,11 @@
         left = jnp.concatenate([packed[:rows], packed[rows:]], axis=1).astype(jnp.bfloat16)
         return jnp.dot(left, wo[chunk], preferred_element_type=jnp.float32)
 
-    def output_step(step, acc):
-        other = neighbour_at(me, step, count)
+    acc = contribution(me)
+    for step in range(1, count):
+        other = partners[step]
         arrival(ctx_all, ctx_send, ctx_recv, other).wait_recv()
-        return acc + contribution(other)
-
-    acc = lax.fori_loop(1, count, output_step, contribution(me))
+        acc = acc + contribution(other)
 
     def pack(array, keep):
         cut = array.shape[1] // 2
@@ -346,8 +345,7 @@
 
     swap.wait_send()
     for step in range(1, count):
-        other = neighbour_at(me, step, count)
-        sq_copy(other).wait_send()
+        other = partners[step]
         part_copy(other).wait_send()
         ctx_copy(other).wait_send()
 
@@ -358,22 +356,24 @@
     width = query_width // count
     kv_width = key_weight.shape[1]
     out_width = w_output.shape[1]
-    packed = (width + 2 * HEAD_SIZE) // 2
+    packed = (width + 2 * HEAD_SIZE) // 2 + HEAD_SIZE
     hbm = pl.BlockSpec(memory_space=pl.ANY)
     vmem = pl.BlockSpec(memory_space=pltpu.VMEM)
     dma = pltpu.SemaphoreType.DMA
     return pl.pallas_call(
         functools.partial(fused_kernel, count),
         out_shape=jax.ShapeDtypeStruct((rows // 2, out_width), jnp.bfloat16),
-        in_specs=[pl.BlockSpec(memory_space=pltpu.SMEM), vmem, vmem, hbm, hbm, hbm, hbm],
+        in_specs=[hbm] * 7,
         out_specs=vmem,
         scratch_shapes=[
+            pltpu.SMEM((rows,), jnp.int32),
+            pltpu.VMEM((rows, depth), jnp.bfloat16),
+            pltpu.VMEM((depth,), jnp.bfloat16),
             pltpu.VMEM((count, depth, width), jnp.bfloat16),
             pltpu.VMEM((depth, 2 * kv_width), jnp.bfloat16),
             pltpu.VMEM((count, width, out_width), jnp.bfloat16),
             pltpu.VMEM((rows, depth), jnp.bfloat16),
             pltpu.VMEM((kv_width // HEAD_SIZE, rows, 2 * HEAD_SIZE), jnp.float32),
-            pltpu.VMEM((count, rows, HEAD_SIZE), jnp.float32),
             pltpu.VMEM((count, 2 * rows, packed), jnp.bfloat16),
             pltpu.VMEM((count, 2 * rows, packed), jnp.bfloat16),
             pltpu.VMEM((2 * rows, packed), jnp.float32),
@@ -383,8 +383,7 @@
             dma((count,)),
             dma((2,)),
             dma((count,)),
-            dma((count,)),
-            dma((count,)),
+            dma((3,)),
             dma((count,)),
             dma((count,)),
             dma((count,)),
@@ -394,7 +393,7 @@
         compiler_params=pltpu.CompilerParams(
             collective_id=0, has_side_effects=True, vmem_limit_bytes=56 * 1024 * 1024
         ),
-    )(positions, tokens, norm_gain.reshape(1, depth), w_query, key_weight, value_weight, w_output)
+    )(positions, tokens, norm_gain, w_query, key_weight, value_weight, w_output)
 
 
 def block(count, cores, tokens, norm_gain, positions, w_query, key_weight, value_weight, w_output):

time: 27.8 us -> 25.1 us (0.903)
  Pallas kernels: 24.9 us -> 23.5 us
  local copies, waits for them, and re-layouts: 2.62 us -> 1.33 us
    pallas_call x1, Pallas kernels: 24.9 us -> 23.5 us  [fused(): pl.pallas_call(functools.partial(fused_kernel, count), out_shape=jax.Shap...]
    reshape x1 -> x0, local copies, waits for them, and re-layouts: 1.29 us -> none  [fused(): norm_gain.reshape(1, depth)]
where the time goes in v2:
time: 25.1 us; the launch traced here: 24.8 us
  Pallas kernels  23.5 us (94%)
  local copies, waits for them, and re-layouts  1.33 us (5%)
    pallas_call x1, Pallas kernels, fused(): pl.pallas_call(functools.partial(fused_kernel, count), out_shape=jax.Shap...  23.5 us
    unnamed x1, local copies, waits for them, and re-layouts  1.33 us

profile of v2, /device:TPU:0, one launch (start us, length us, event | category | flops | bytes accessed | tf_op | source)
XLA Modules:
  0.0 24.8 jit_solution(4915965868438164798)
XLA Ops:
  0.0 23.5 %shard_map.73 = bf16[4,2048]{1,0:T(4,128)(2,1)} custom-call(s32[8]{0:T(128)} %pos_hbm.1, bf16[8,2048]{1,0:T(8,128)(2,1)} %tok_hbm.1, bf16[2048]{0:T(1024)(128)(2,1)} %gain_hbm.1, bf16[2048,4096]{1,0:T(8,128)(2,1)} %wq_hbm.1, bf16[2048,256]{1,0:T(8,128)(2,1)} %wk_hbm.1, bf16[2048,256]{1,0:T(8,128)(2,1)} %wv_hbm.1, bf16[4096,2048]{1,0:T(8,128)(2,1)} %wo_hbm.1), custom_call_target="tpu_custom_call" | custom-call | tf_op jit(solution)/shard_map/pallas_call | solution.py:363
  23.5 1.3 %copy.9 = bf16[4,2048]{1,0:T(4,128)(2,1)} copy(bf16[4,2048]{1,0:T(4,128)(2,1)} %shard_map.73) | data formatting | bytes 32768

commit v3 on v2

--- a/solution.py
+++ b/solution.py
@@ -306,16 +306,18 @@
         ctx_copy(partners[step]).start()
 
     def contribution(chunk):
-        wo_copy(chunk).wait()
         packed = ctx_all[chunk].astype(jnp.float32)
         left = jnp.concatenate([packed[:rows], packed[rows:]], axis=1).astype(jnp.bfloat16)
         return jnp.dot(left, wo[chunk], preferred_element_type=jnp.float32)
 
+    wo_copy(me).wait()
     acc = contribution(me)
-    for step in range(1, count):
-        other = partners[step]
-        arrival(ctx_all, ctx_send, ctx_recv, other).wait_recv()
-        acc = acc + contribution(other)
+    for group in (partners[1 : count // 2], partners[count // 2 :]):
+        for other in group:
+            wo_copy(other).wait()
+            arrival(ctx_all, ctx_send, ctx_recv, other).wait_recv()
+        for other in group:
+            acc = acc + contribution(other)
 
     def pack(array, keep):
         cut = array.shape[1] // 2

time: 25.1 us -> 25.6 us (1.020)
  Pallas kernels: 23.5 us -> 24 us
    pallas_call x1, Pallas kernels: 23.5 us -> 24 us  [fused(): pl.pallas_call(functools.partial(fused_kernel, count), out_shape=jax.Shap...]
where the time goes in v3:
time: 25.6 us; the launch traced here: 25.3 us
  Pallas kernels  24 us (94%)
  local copies, waits for them, and re-layouts  1.33 us (5%)
    pallas_call x1, Pallas kernels, fused(): pl.pallas_call(functools.partial(fused_kernel, count), out_shape=jax.Shap...  24 us
    unnamed x1, local copies, waits for them, and re-layouts  1.33 us

profile of v3, /device:TPU:0, one launch (start us, length us, event | category | flops | bytes accessed | tf_op | source)
XLA Modules:
  0.0 25.3 jit_solution(5376862576493106854)
XLA Ops:
  0.0 24.0 %shard_map.73 = bf16[4,2048]{1,0:T(4,128)(2,1)} custom-call(s32[8]{0:T(128)} %pos_hbm.1, bf16[8,2048]{1,0:T(8,128)(2,1)} %tok_hbm.1, bf16[2048]{0:T(1024)(128)(2,1)} %gain_hbm.1, bf16[2048,4096]{1,0:T(8,128)(2,1)} %wq_hbm.1, bf16[2048,256]{1,0:T(8,128)(2,1)} %wk_hbm.1, bf16[2048,256]{1,0:T(8,128)(2,1)} %wv_hbm.1, bf16[4096,2048]{1,0:T(8,128)(2,1)} %wo_hbm.1), custom_call_target="tpu_custom_call" | custom-call | tf_op jit(solution)/shard_map/pallas_call | solution.py:365
  24.0 1.3 %copy.9 = bf16[4,2048]{1,0:T(4,128)(2,1)} copy(bf16[4,2048]{1,0:T(4,128)(2,1)} %shard_map.73) | data formatting | bytes 32768
